TPU v7x, 32 devices: a whole 2x2x4 slice. The times are simulated.
32 devices in a mesh: group: 4 (over y, core), blk: 8 (over z, x).
Axes of the slice: x: 2, y: 2, z: 4, core: 2. Of those that a mesh axis runs over, the one named last changes fastest.
Arguments:
- queries: bfloat16 [2048, 32, 128], P('blk'), may hold values from -8 to 8
- doc_blocks: bfloat16 [4, 128, 128, 128], P('group', 'blk'), may hold values from -2 to 2
- doc_len: int32 [4, 128], P('group', 'blk'), may hold values from 96 to 128
- candidates: int32 [4, 8, 4, 8], P('group', 'blk'), may hold values from 0 to 17, as said below
- cand_count: int32 [4, 8, 4], P('group', 'blk'), may hold values from 2 to 8, as said below
- hot_owned: int32 [4, 8, 1], P('group', 'blk'), may hold values from 0 to 15
- hot_taken: int32 [4, 8, 2], P('group', 'blk'), may hold values from 0 to 7, as said below
Outputs:
- top_scores: float32 [2048, 16], P('blk')
Inputs may be any that keep to these rules, and one draw needn't show every extreme that they name: `candidates`: slots below 16 name a device's own blocks, the others its hot copies; entries at or past the hop's count are ignored. `cand_count`: every query block has 8 live candidates at one or more of its hops. `hot_taken`: entries are hot pool indices of the same group; every pool entry is held by some device.
All inputs are finite; a program needn't handle non-finite values.
Results may differ from a plain program's by a relative error of at most 0.0003.
Values may be sent and summed in bfloat16 or wider, within the bound.
A program may use at most 64 MiB of HBM per device.

v0:
```python
import jax
import jax.numpy as jnp
from jax import lax
from jax.sharding import PartitionSpec as P

QTOK = 32
TOPK = 16
MASKED_SCORE = -1e30


def shifted(x, axis, by):
    peers = lax.axis_size(axis)
    return lax.ppermute(x, axis, [(i, (i + by) % peers) for i in range(peers)])


def maxsim(query_part, blocks, lengths):

    def single(element):
        doc_block, length = element
        scores = lax.dot_general(
            query_part, doc_block, (((1,), (1,)), ((), ())), preferred_element_type=jnp.float32
        )
        keep_mask = jnp.arange(doc_block.shape[0], dtype=jnp.int32) < length
        scores = jnp.where(keep_mask[None, :], scores, MASKED_SCORE)
        best_rows = jnp.max(scores, axis=1).reshape(-1, QTOK)
        return jnp.sum(best_rows, axis=1) / QTOK

    return lax.map(single, (blocks, lengths)).T


def masked_scores(query_part, chosen, chosen_len, live_count):
    scores = maxsim(query_part, chosen, chosen_len)
    keep_mask = jnp.arange(chosen.shape[0], dtype=jnp.int32) < live_count
    return jnp.where(keep_mask[None, :], scores, MASKED_SCORE)


def hop_scores(query_part, blocks, lengths, slots, live_count):
    chosen = jnp.take(blocks, slots, axis=0)
    chosen_len = jnp.take(lengths, slots, axis=0)
    return masked_scores(query_part, chosen, chosen_len, live_count)


def on_device(queries, doc_blocks, doc_len, candidates, cand_count, hot_owned, hot_taken):
    lengths_all, cand_all, count_all, taken_all, owned_all = (
        lax.all_gather(doc_len, "blk", axis=1, tiled=True),
        lax.all_gather(candidates, "blk", axis=1, tiled=True),
        lax.all_gather(cand_count, "blk", axis=1, tiled=True),
        lax.all_gather(hot_taken, "blk", axis=1, tiled=True),
        lax.all_gather(hot_owned, "blk", axis=1, tiled=True),
    )
    shards = lax.axis_size("blk")
    position = lax.axis_index("blk")
    per_dev = doc_blocks.shape[1]
    hot_pub = hot_owned.shape[2]
    hot_dev = hot_taken.shape[2]
    hop_total = candidates.shape[2]
    owner_dev = taken_all[0] // hot_pub
    member = taken_all[0] % hot_pub
    hot_ids = owner_dev * per_dev + owned_all[0][owner_dev, member]
    own_ids = (
        jnp.arange(shards, dtype=jnp.int32)[:, None] * per_dev
        + jnp.arange(per_dev, dtype=jnp.int32)[None, :]
    )
    ext_len_all = jnp.take(lengths_all[0], jnp.concatenate([own_ids, hot_ids], axis=1), axis=0)
    local_blocks = doc_blocks[0]
    published = jnp.take(local_blocks, hot_owned[0, 0], axis=0)
    taken_here = hot_taken[0, 0]
    empty_blocks = jnp.zeros((hot_dev,) + local_blocks.shape[1:], local_blocks.dtype)
    shard_piece = lax.all_gather(published, "blk", axis=0, tiled=True)
    row_count = shard_piece.shape[0]
    inside = (taken_here >= 0) & (taken_here < row_count)
    picked = jnp.take(shard_piece, jnp.clip(taken_here, 0, row_count - 1), axis=0)
    hot_blocks = jnp.where(inside[:, None, None], picked, empty_blocks)
    ext_blocks = jnp.concatenate([local_blocks, hot_blocks], axis=0)
    query_rows = queries.reshape(-1, queries.shape[2])
    score_parts = []
    visiting = query_rows
    for hop_number in range(hop_total):
        if hop_number > 0:
            visiting = shifted(visiting, "blk", 1)
        home_dev = (position - hop_number) % shards
        scores = hop_scores(
            visiting,
            ext_blocks,
            ext_len_all[position],
            cand_all[0, home_dev, hop_number],
            count_all[0, home_dev, hop_number],
        )
        if hop_number > 0:
            scores = shifted(scores, "blk", -hop_number)
        score_parts.append(scores)
    combined = jnp.concatenate(score_parts, axis=1)
    every_group = lax.all_gather(combined, "group", axis=1, tiled=True)
    top_values = lax.top_k(every_group, TOPK)[0]
    return top_values


def solution(mesh):
    return jax.shard_map(
        on_device,
        mesh=mesh,
        in_specs=(
            P("blk", None, None),
            P("group", "blk", None, None),
            P("group", "blk"),
            P("group", "blk", None, None),
            P("group", "blk", None),
            P("group", "blk", None),
            P("group", "blk", None),
        ),
        out_specs=P("blk", None),
        check_vma=False,
    )
```

profile of v0, /device:TPU:0, one launch (start us, length us, event | category | flops | bytes accessed | tf_op | source)
XLA Modules:
  0.0 288.4 jit_solution(9362428100582840750)
XLA Ops:
  0.0 2.9 %collective-permute-start = (bf16[8192,128]{1,0:T(8,128)(2,1)}, bf16[8192,128]{1,0:T(8,128)(2,1)}, u32[]{:S(2)}, u32[]{:S(2)}) collective-permute-start(bf16[8192,128]{1,0:T(8,128)(2,1)} %bitcast.140), channel_id=1, source_target_pairs={{0,1},{1,2},{2,3},{3,4},{4,5},{5,6},{6,7},{7,0},{8,9},{9,10},{10,1... | collective-permute-start | bytes 6291464 | tf_op jit(solution)/shard_map/ppermute | solution.py:13
  5.6 57.3 %all_gather.22 = s32[1,8,2]{2,0,1:T(1,128)S(1)} all-gather(s32[1,1,2]{2,0,1:T(1,128)} %bitcast.138), channel_id=1, replica_groups=mesh['group'=4,'blk'=8] {'blk'}, dimensions={1}, use_global_device_ids=true | all-gather | bytes 72 | tf_op jit(solution)/shard_map/all_gather | solution.py:48
  63.2 1.2 dynamic-slice.5
  65.8 0.8 bitcast_dynamic-update-slice_fusion
  66.6 6.9 %all-reduce.3 = (s32[128]{0:T(128)S(1)}, s32[8]{0:T(128)S(1)}) all-reduce(s32[128]{0:T(128)S(1)} %bitcast_dynamic-update-slice_fusion, s32[8]{0:T(128)S(1)} %bitcast_dynamic-update-slice_fusion.1), channel_id=1, replica_groups=mesh['group'=4,'blk'=8] {'blk'}, use_global_device_ids=true, to_apply=%add.2 | all-reduce | flops 136 | bytes 1088 | tf_op jit(solution)/shard_map/squeeze | solution.py:64
  74.7 1.6 gather_fusion.1
  76.3 27.8 %all_gather.25 = s32[1,8,4,8]{3,2,0,1:T(4,128)S(1)} all-gather(s32[1,1,4,8]{3,2,0,1:T(4,128)S(1)} %bitcast.137), channel_id=1, replica_groups=mesh['group'=4,'blk'=8] {'blk'}, dimensions={1}, use_global_device_ids=true | all-gather | bytes 1152 | tf_op jit(solution)/shard_map/all_gather | solution.py:46
  105.0 30.8 %all-gather = bf16[8,1,128,128]{3,2,1,0:T(8,128)(2,1)S(1)} all-gather(bf16[1,1,128,128]{3,2,1,0:T(8,128)(2,1)S(1)} %dynamic-slice_select_fusion), channel_id=2, replica_groups=mesh['group'=4,'blk'=8] {'blk'}, dimensions={0}, use_global_device_ids=true | all-gather | bytes 294912 | tf_op jit(solution)/shard_map/all_gather | solution.py:69
  137.3 18.0 %while.41 = (s32[]{:T(128)}, f32[8,256]{1,0:T(8,128)S(1)}, s32[8]{0:T(128)S(1)}, bf16[8,128,128]{2,1,0:T(8,128)(2,1)S(1)}, bf16[8192,128]{1,0:T(8,128)(2,1)S(1)}, /*index=5*/s32[]{:T(128)}, f32[]{:T(128)}, s32[]{:T(128)}) while((s32[]{:T(128)}, f32[8,256]{1,0:T(8,128)S(1)}, s32[8]{0:T(128)S(1)}, bf16[8,128,128]{2,1,0:T(8,128)(2,1)S(1)}, ...), condition=%wide.region_3.6_spmd, body=%wide.region_0.5_spmd.sunk | while | flops 270532736 | bytes 2266873 | solution.py:28
  138.5 0.7 fusion.43
  140.8 0.7 fusion.43
  143.0 0.7 fusion.43
  145.3 0.7 fusion.43
  147.5 0.7 fusion.43
  149.8 0.7 fusion.43
  152.0 0.7 fusion.43
  154.3 0.7 fusion.43
  159.1 17.7 %all_gather.21 = s32[1,8,4]{2,0,1:T(1,128)S(1)} all-gather(s32[1,1,4]{2,0,1:T(1,128)S(1)} %bitcast.139), channel_id=1, replica_groups=mesh['group'=4,'blk'=8] {'blk'}, dimensions={1}, use_global_device_ids=true | all-gather | bytes 144 | tf_op jit(solution)/shard_map/all_gather | solution.py:47
  180.8 31.7 %while.42 = (s32[]{:T(128)}, f32[8,256]{1,0:T(8,128)S(1)}, s32[8]{0:T(128)S(1)}, bf16[8,128,128]{2,1,0:T(8,128)(2,1)S(1)}, bf16[8192,128]{1,0:T(8,128)(2,1)}, /*index=5*/s32[]{:T(128)}, f32[]{:T(128)}, s32[]{:T(128)}) while((s32[]{:T(128)}, f32[8,256]{1,0:T(8,128)S(1)}, s32[8]{0:T(128)S(1)}, bf16[8,128,128]{2,1,0:T(8,128)(2,1)S(1)}, ...), condition=%wide.region_7.10_spmd, body=%wide.region_4.9_spmd.sunk | while | flops 270532736 | bytes 2266873 | solution.py:28
  181.5 0.7 iota_compare_fusion.13
  182.2 2.3 fusion.46
  185.5 0.7 iota_compare_fusion.13
  186.2 2.3 fusion.46
  189.4 0.7 iota_compare_fusion.13
  190.1 2.3 fusion.46
  193.4 0.7 iota_compare_fusion.13
  194.1 2.3 fusion.46
  197.4 0.7 iota_compare_fusion.13
  198.1 2.3 fusion.46
  201.3 0.7 iota_compare_fusion.13
  202.0 2.3 fusion.46
  205.3 0.7 iota_compare_fusion.13
  206.0 2.3 fusion.46
  209.3 0.7 iota_compare_fusion.13
  210.0 2.3 fusion.46
  212.6 4.1 %collective-permute-start.1 = (f32[256,8]{0,1:T(8,128)S(1)}, f32[256,8]{0,1:T(8,128)S(1)}, u32[]{:S(2)}, u32[]{:S(2)}) collective-permute-start(f32[256,8]{0,1:T(8,128)S(1)} %select_bitcast_fusion.2), channel_id=1, source_target_pairs={{0,7},{1,0},{2,1},{3,2},{4,3},{5,4},{6,5},{7,6},{8,15},{9,8},{10,9... | collective-permute-start | bytes 24584 | tf_op jit(solution)/shard_map/ppermute | solution.py:13
  216.7 2.8 collective-permute-done.2
  219.5 31.7 %while.43 = (s32[]{:T(128)}, f32[8,256]{1,0:T(8,128)S(1)}, s32[8]{0:T(128)S(1)}, bf16[8,128,128]{2,1,0:T(8,128)(2,1)S(1)}, bf16[8192,128]{1,0:T(8,128)(2,1)}, /*index=5*/s32[]{:T(128)}, f32[]{:T(128)}, s32[]{:T(128)}) while((s32[]{:T(128)}, f32[8,256]{1,0:T(8,128)S(1)}, s32[8]{0:T(128)S(1)}, bf16[8,128,128]{2,1,0:T(8,128)(2,1)S(1)}, ...), condition=%wide.region_11.14_spmd, body=%wide.region_8.13_spmd.sunk | while | flops 270532736 | bytes 2266873 | solution.py:28
  220.2 0.7 iota_compare_fusion.14
  220.9 2.3 fusion.49
  224.2 0.7 iota_compare_fusion.14
  224.8 2.3 fusion.49
  228.8 2.3 fusion.49
  232.8 2.3 fusion.49
  236.0 0.7 iota_compare_fusion.14
  236.7 2.3 fusion.49
  240.0 0.7 iota_compare_fusion.14
  240.7 2.3 fusion.49
  244.7 2.3 fusion.49
  248.6 2.3 fusion.49
  251.3 4.3 %collective-permute-done.4 = bf16[8192,128]{1,0:T(8,128)(2,1)S(1)} collective-permute-done((bf16[8192,128]{1,0:T(8,128)(2,1)}, bf16[8192,128]{1,0:T(8,128)(2,1)S(1)}, u32[]{:S(2)}, u32[]{:S(2)}) %collective-permute-start.4) | collective-permute-done | bytes 2097184 | tf_op jit(solution)/shard_map/ppermute | solution.py:13
  255.6 18.9 %while.44 = (s32[]{:T(128)}, f32[8,256]{1,0:T(8,128)S(1)}, s32[8]{0:T(128)S(1)}, bf16[8,128,128]{2,1,0:T(8,128)(2,1)S(1)}, bf16[8192,128]{1,0:T(8,128)(2,1)S(1)}, /*index=5*/s32[]{:T(128)}, f32[]{:T(128)}, s32[]{:T(128)}) while((s32[]{:T(128)}, f32[8,256]{1,0:T(8,128)S(1)}, s32[8]{0:T(128)S(1)}, bf16[8,128,128]{2,1,0:T(8,128)(2,1)S(1)}, ...), condition=%wide.region_15.18_spmd, body=%wide.region_12.17_spmd.sunk | while | flops 270532736 | bytes 2266873 | solution.py:28
  256.3 0.7 iota_compare_fusion.15
  257.0 0.7 fusion.52
  259.3 0.7 fusion.52
  261.7 0.7 fusion.52
  264.1 0.7 fusion.52
  266.4 0.7 fusion.52
  268.8 0.7 fusion.52
  271.2 0.7 fusion.52
  273.5 0.7 fusion.52
  274.7 4.5 %collective-permute-done.5 = f32[256,8]{0,1:T(8,128)S(1)} collective-permute-done((f32[256,8]{0,1:T(8,128)S(1)}, f32[256,8]{0,1:T(8,128)S(1)}, u32[]{:S(2)}, u32[]{:S(2)}) %collective-permute-start.5) | collective-permute-done | bytes 8224 | tf_op jit(solution)/shard_map/ppermute | solution.py:13
  279.2 5.4 %all_gather.27 = f32[256,128]{0,1:T(8,128)S(1)} all-gather(f32[256,32]{0,1:T(8,128)S(1)} %pad_maximum_fusion.1), channel_id=1, replica_groups=mesh['group'=4,'blk'=8] {'group'}, dimensions={1}, use_global_device_ids=true | all-gather | bytes 163840 | tf_op jit(solution)/shard_map/all_gather | solution.py:93
  284.6 3.0 %top_k.9 = (f32[256,128]{0,1:T(8,128)S(1)}, s32[256,128]{0,1:T(8,128)}) sort(f32[256,128]{0,1:T(8,128)S(1)} %all_gather.27, s32[256,128]{0,1:T(8,128)S(1)} %iota.59.clone), dimensions={1}, to_apply=%region_16.19 | sort | flops 491520 | bytes 524288 | tf_op jit(solution)/shard_map/top_k | solution.py:94
  (259 shorter events, 56.3 us)
Async XLA Ops:
  0.0 180.2 %collective-permute-start = (bf16[8192,128]{1,0:T(8,128)(2,1)}, bf16[8192,128]{1,0:T(8,128)(2,1)}, u32[]{:S(2)}, u32[]{:S(2)}) collective-permute-start(bf16[8192,128]{1,0:T(8,128)(2,1)} %bitcast.140), channel_id=1, source_target_pairs={{0,1},{1,2},{2,3},{3,4},{4,5},{5,6},{6,7},{7,0},{8,9},{9,10},{10,1... | collective-permute-start | bytes 6291464 | tf_op jit(solution)/shard_map/ppermute | solution.py:13
  74.7 1.7 copy-start.1
  74.7 30.3 %copy-start = (bf16[1,16,128,128]{3,2,1,0:T(8,128)(2,1)S(1)}, bf16[1,16,128,128]{3,2,1,0:T(8,128)(2,1)}, u32[]{:S(2)}) copy-start(bf16[1,16,128,128]{3,2,1,0:T(8,128)(2,1)} %param.20) | copy-start | bytes 1572868
  76.2 61.0 %copy-start.3 = (bf16[256,32,128]{2,1,0:T(8,128)(2,1)S(1)}, bf16[256,32,128]{2,1,0:T(8,128)(2,1)}, u32[]{:S(2)}) copy-start(bf16[256,32,128]{2,1,0:T(8,128)(2,1)} %param.19) | copy-start | bytes 6291460
  155.3 3.8 %copy-start.2 = (s32[1,1,4]{2,1,0:T(1,128)S(1)}, s32[1,1,4]{2,1,0:T(1,128)}, u32[]{:S(2)}) copy-start(s32[1,1,4]{2,1,0:T(1,128)} %param.23) | copy-start | bytes 52
  180.2 39.3 %collective-permute-start.2 = (bf16[8192,128]{1,0:T(8,128)(2,1)}, bf16[8192,128]{1,0:T(8,128)(2,1)}, u32[]{:S(2)}, u32[]{:S(2)}) collective-permute-start(bf16[8192,128]{1,0:T(8,128)(2,1)} %collective-permute-done), channel_id=1, source_target_pairs={{0,1},{1,2},{2,3},{3,4},{4,5},{5,6},{6,7},{7,0},{8,9},{9,10},{10,1... | collective-permute-start | bytes 6291464 | tf_op jit(solution)/shard_map/ppermute | solution.py:13
  212.6 62.1 %collective-permute-start.1 = (f32[256,8]{0,1:T(8,128)S(1)}, f32[256,8]{0,1:T(8,128)S(1)}, u32[]{:S(2)}, u32[]{:S(2)}) collective-permute-start(f32[256,8]{0,1:T(8,128)S(1)} %select_bitcast_fusion.2), channel_id=1, source_target_pairs={{0,7},{1,0},{2,1},{3,2},{4,3},{5,4},{6,5},{7,6},{8,15},{9,8},{10,9... | collective-permute-start | bytes 24584 | tf_op jit(solution)/shard_map/ppermute | solution.py:13
  219.5 36.1 %collective-permute-start.4 = (bf16[8192,128]{1,0:T(8,128)(2,1)}, bf16[8192,128]{1,0:T(8,128)(2,1)S(1)}, u32[]{:S(2)}, u32[]{:S(2)}) collective-permute-start(bf16[8192,128]{1,0:T(8,128)(2,1)} %collective-permute-done.2), channel_id=1, source_target_pairs={{0,1},{1,2},{2,3},{3,4},{4,5},{5,6},{6,7},{7,0},{8,9},{9,10},{10,1... | collective-permute-start | bytes 6291464 | tf_op jit(solution)/shard_map/ppermute | solution.py:13
  251.3 23.4 %collective-permute-start.3 = (f32[256,8]{0,1:T(8,128)S(1)}, f32[256,8]{0,1:T(8,128)S(1)}, u32[]{:S(2)}, u32[]{:S(2)}) collective-permute-start(f32[256,8]{0,1:T(8,128)S(1)} %select_bitcast_fusion.1), channel_id=1, source_target_pairs={{0,6},{1,7},{2,0},{3,1},{4,2},{5,3},{6,4},{7,5},{8,14},{9,15},{10,... | collective-permute-start | bytes 24584 | tf_op jit(solution)/shard_map/ppermute | solution.py:13
  274.6 4.5 %collective-permute-start.5 = (f32[256,8]{0,1:T(8,128)S(1)}, f32[256,8]{0,1:T(8,128)S(1)}, u32[]{:S(2)}, u32[]{:S(2)}) collective-permute-start(f32[256,8]{0,1:T(8,128)S(1)} %select_bitcast_fusion), channel_id=1, source_target_pairs={{0,5},{1,6},{2,7},{3,0},{4,1},{5,2},{6,3},{7,4},{8,13},{9,14},{10,... | collective-permute-start | bytes 24584 | tf_op jit(solution)/shard_map/ppermute | solution.py:13
where the time goes:
time: 290 us; the launch traced here: 288 us
  blocking collectives  146 us (50%)
  matrix products  48.6 us (17%)
  local copies, waits for them, and re-layouts  37.1 us (13%)
  other arithmetic  34 us (12%)
  waiting for transfers between devices  11.5 us (4%)
  starting transfers between devices  7.72 us (3%)
    all_gather x1, blocking collectives, on_device(): lax.all_gather(hot_taken, 'blk', axis=1, tiled=True)  57.3 us
    dot_general x32, matrix products, single(): lax.dot_general(query_part, doc_block, (((1,), (1,)), ((), ())), preferre...  48.6 us
    all_gather x1, blocking collectives, on_device(): shard_piece = lax.all_gather(published, 'blk', axis=0, tiled=True)  30.8 us
    all_gather x1, blocking collectives, on_device(): lax.all_gather(candidates, 'blk', axis=1, tiled=True)  27.8 us
    lt x32, other arithmetic, single(): keep_mask = jnp.arange(doc_block.shape[0], dtype=jnp.int32) < length  21.8 us
    dynamic_slice x32, local copies, waits for them, and re-layouts, maxsim(): return lax.map(single, (blocks, lengths)).T  20.7 us
    all_gather x1, blocking collectives, on_device(): lax.all_gather(cand_count, 'blk', axis=1, tiled=True)  17.7 us
    ppermute x6, waiting for transfers between devices, shifted(): return lax.ppermute(x, axis, [(i, (i + by) % peers) for i in range(peers)])  11.5 us
  transfers between devices with their start and end apart: 6, of which 3 were waited for; matrix products, arithmetic and copies ran while one was open for 40% of the time, Pallas kernels for 0%

commit v1 on v0

--- a/solution.py
+++ b/solution.py
@@ -66,7 +66,12 @@
     published = jnp.take(local_blocks, hot_owned[0, 0], axis=0)
     taken_here = hot_taken[0, 0]
     empty_blocks = jnp.zeros((hot_dev,) + local_blocks.shape[1:], local_blocks.dtype)
-    shard_piece = lax.all_gather(published, "blk", axis=0, tiled=True)
+    ring = [published]
+    for hop in range(7):
+        ring.append(lax.ppermute(ring[-1], "blk", [(dev, (dev + 1) % 8) for dev in range(8)]))
+    shard_piece = jnp.roll(
+        jnp.concatenate(ring[::-1], axis=0), (lax.axis_index("blk") + 1) * ring[0].shape[0], axis=0
+    )
     row_count = shard_piece.shape[0]
     inside = (taken_here >= 0) & (taken_here < row_count)
     picked = jnp.take(shard_piece, jnp.clip(taken_here, 0, row_count - 1), axis=0)

time: 290 us -> 294 us (1.014)
  waiting for transfers between devices: 11.5 us -> 40.5 us
  blocking collectives: 146 us -> 119 us
    all_gather x1 -> x0, blocking collectives: 30.8 us -> none  [on_device(): shard_piece = lax.all_gather(published, 'blk', axis=0, tiled=True)]
    ppermute x0 -> x7, waiting for transfers between devices: none -> 29.6 us  [on_device(): lax.ppermute(ring[-1], 'blk', [(dev, (dev + 1) % 8) for dev in range(8)])]
    ppermute x0 -> x7, starting transfers between devices: none -> 3.94 us  [on_device(): lax.ppermute(ring[-1], 'blk', [(dev, (dev + 1) % 8) for dev in range(8)])]
    all_gather x1, blocking collectives: 17.7 us -> 20.9 us  [on_device(): lax.all_gather(cand_count, 'blk', axis=1, tiled=True)]
  transfers between devices with their start and end apart: 6 -> 13, of which waited for: 3 -> 8; matrix products, arithmetic and copies ran while one was open for 40% -> 39% of each run, Pallas kernels for 0% -> 0%
where the time goes in v1:
time: 294 us; the launch traced here: 293 us
  blocking collectives  119 us (40%)
  matrix products  48.8 us (17%)
  waiting for transfers between devices  40.5 us (14%)
  local copies, waits for them, and re-layouts  37.5 us (13%)
  other arithmetic  33.3 us (11%)
  starting transfers between devices  10.2 us (3%)
    all_gather x1, blocking collectives, on_device(): lax.all_gather(hot_taken, 'blk', axis=1, tiled=True)  58.3 us
    dot_general x32, matrix products, single(): lax.dot_general(query_part, doc_block, (((1,), (1,)), ((), ())), preferre...  48.8 us
    ppermute x7, waiting for transfers between devices, on_device(): lax.ppermute(ring[-1], 'blk', [(dev, (dev + 1) % 8) for dev in range(8)])  29.6 us
    all_gather x1, blocking collectives, on_device(): lax.all_gather(candidates, 'blk', axis=1, tiled=True)  27.2 us
    lt x32, other arithmetic, single(): keep_mask = jnp.arange(doc_block.shape[0], dtype=jnp.int32) < length  21.6 us
    all_gather x1, blocking collectives, on_device(): lax.all_gather(cand_count, 'blk', axis=1, tiled=True)  20.9 us
    dynamic_slice x32, local copies, waits for them, and re-layouts, maxsim(): return lax.map(single, (blocks, lengths)).T  20.7 us
    ppermute x6, waiting for transfers between devices, shifted(): return lax.ppermute(x, axis, [(i, (i + by) % peers) for i in range(peers)])  10.9 us
  transfers between devices with their start and end apart: 13, of which 8 were waited for; matrix products, arithmetic and copies ran while one was open for 39% of the time, Pallas kernels for 0%

profile of v1, /device:TPU:0, one launch (start us, length us, event | category | flops | bytes accessed | tf_op | source)
XLA Modules:
  0.0 293.1 jit_solution(14751393252406588020)
XLA Ops:
  0.7 0.8 select_bitcast_fusion
  1.4 2.9 %collective-permute-start = (bf16[1,128,128]{2,1,0:T(8,128)(2,1)S(1)}, bf16[1,128,128]{2,1,0:T(8,128)(2,1)S(1)}, u32[]{:S(2)}, u32[]{:S(2)}) collective-permute-start(bf16[1,128,128]{2,1,0:T(8,128)(2,1)S(1)} %select_bitcast_fusion), channel_id=1, source_target_pairs={{0,1},{1,2},{2,3},{3,4},{4,5},{5,6},{6,7},{7,0},{8,9},{9,10},{10,1... | collective-permute-start | bytes 98312 | tf_op jit(solution)/shard_map/ppermute | solution.py:71
  4.4 1.5 collective-permute-start.7
  6.6 58.3 %all_gather.19 = s32[1,8,2]{2,0,1:T(1,128)S(1)} all-gather(s32[1,1,2]{2,0,1:T(1,128)} %bitcast.142), channel_id=1, replica_groups=mesh['group'=4,'blk'=8] {'blk'}, dimensions={1}, use_global_device_ids=true | all-gather | bytes 72 | tf_op jit(solution)/shard_map/all_gather | solution.py:48
  65.1 1.2 dynamic-slice.5
  67.7 0.8 bitcast_dynamic-update-slice_fusion
  68.5 7.5 %all-reduce.3 = (s32[128]{0:T(128)S(1)}, s32[8]{0:T(128)S(1)}) all-reduce(s32[128]{0:T(128)S(1)} %bitcast_dynamic-update-slice_fusion, s32[8]{0:T(128)S(1)} %bitcast_dynamic-update-slice_fusion.1), channel_id=1, replica_groups=mesh['group'=4,'blk'=8] {'blk'}, use_global_device_ids=true, to_apply=%add.2 | all-reduce | flops 136 | bytes 1088 | tf_op jit(solution)/shard_map/squeeze | solution.py:64
  77.2 1.6 gather_fusion.1
  78.9 27.2 %all_gather.22 = s32[1,8,4,8]{3,2,0,1:T(4,128)S(1)} all-gather(s32[1,1,4,8]{3,2,0,1:T(4,128)S(1)} %bitcast.141), channel_id=1, replica_groups=mesh['group'=4,'blk'=8] {'blk'}, dimensions={1}, use_global_device_ids=true | all-gather | bytes 1152 | tf_op jit(solution)/shard_map/all_gather | solution.py:46
  108.9 1.0 collective-permute-start.1
  109.9 5.7 %collective-permute-done.1 = bf16[1,128,128]{2,1,0:T(8,128)(2,1)S(1)} collective-permute-done((bf16[1,128,128]{2,1,0:T(8,128)(2,1)S(1)}, bf16[1,128,128]{2,1,0:T(8,128)(2,1)S(1)}, u32[]{:S(2)}, u32[]{:S(2)}) %collective-permute-start.1) | collective-permute-done | bytes 32800 | tf_op jit(solution)/shard_map/ppermute | solution.py:71
  115.6 20.9 %all_gather.18 = s32[1,8,4]{2,0,1:T(1,128)S(1)} all-gather(s32[1,1,4]{2,0,1:T(1,128)S(1)} %bitcast.143), channel_id=1, replica_groups=mesh['group'=4,'blk'=8] {'blk'}, dimensions={1}, use_global_device_ids=true | all-gather | bytes 144 | tf_op jit(solution)/shard_map/all_gather | solution.py:47
  137.8 6.0 %collective-permute-done.3 = bf16[1,128,128]{2,1,0:T(8,128)(2,1)S(1)} collective-permute-done((bf16[1,128,128]{2,1,0:T(8,128)(2,1)S(1)}, bf16[1,128,128]{2,1,0:T(8,128)(2,1)S(1)}, u32[]{:S(2)}, u32[]{:S(2)}) %collective-permute-start.3) | collective-permute-done | bytes 32800 | tf_op jit(solution)/shard_map/ppermute | solution.py:71
  144.3 6.0 %collective-permute-done.4 = bf16[1,128,128]{2,1,0:T(8,128)(2,1)S(1)} collective-permute-done((bf16[1,128,128]{2,1,0:T(8,128)(2,1)S(1)}, bf16[1,128,128]{2,1,0:T(8,128)(2,1)S(1)}, u32[]{:S(2)}, u32[]{:S(2)}) %collective-permute-start.4) | collective-permute-done | bytes 32800 | tf_op jit(solution)/shard_map/ppermute | solution.py:71
  150.9 6.1 %collective-permute-done.5 = bf16[1,128,128]{2,1,0:T(8,128)(2,1)S(1)} collective-permute-done((bf16[1,128,128]{2,1,0:T(8,128)(2,1)S(1)}, bf16[1,128,128]{2,1,0:T(8,128)(2,1)S(1)}, u32[]{:S(2)}, u32[]{:S(2)}) %collective-permute-start.5) | collective-permute-done | bytes 32800 | tf_op jit(solution)/shard_map/ppermute | solution.py:71
  157.6 6.0 %collective-permute-done.6 = bf16[1,128,128]{2,1,0:T(8,128)(2,1)S(1)} collective-permute-done((bf16[1,128,128]{2,1,0:T(8,128)(2,1)S(1)}, bf16[1,128,128]{2,1,0:T(8,128)(2,1)S(1)}, u32[]{:S(2)}, u32[]{:S(2)}) %collective-permute-start.6) | collective-permute-done | bytes 32800 | tf_op jit(solution)/shard_map/ppermute | solution.py:71
  165.3 17.8 %while.41 = (s32[]{:T(128)}, f32[8,256]{1,0:T(8,128)S(1)}, s32[8]{0:T(128)S(1)}, bf16[8,128,128]{2,1,0:T(8,128)(2,1)S(1)}, bf16[8192,128]{1,0:T(8,128)(2,1)S(1)}, /*index=5*/s32[]{:T(128)}, f32[]{:T(128)}, s32[]{:T(128)}) while((s32[]{:T(128)}, f32[8,256]{1,0:T(8,128)S(1)}, s32[8]{0:T(128)S(1)}, bf16[8,128,128]{2,1,0:T(8,128)(2,1)S(1)}, ...), condition=%wide.region_3.6_spmd, body=%wide.region_0.5_spmd.sunk | while | flops 270532736 | bytes 2266873 | solution.py:28
  166.5 0.7 fusion.43
  168.7 0.7 fusion.43
  171.0 0.7 fusion.43
  173.2 0.7 fusion.43
  175.4 0.7 fusion.43
  177.7 0.7 fusion.43
  179.9 0.7 fusion.43
  182.1 0.7 fusion.43
  185.3 31.8 %while.42 = (s32[]{:T(128)}, f32[8,256]{1,0:T(8,128)S(1)}, s32[8]{0:T(128)S(1)}, bf16[8,128,128]{2,1,0:T(8,128)(2,1)S(1)}, bf16[8192,128]{1,0:T(8,128)(2,1)}, /*index=5*/s32[]{:T(128)}, f32[]{:T(128)}, s32[]{:T(128)}) while((s32[]{:T(128)}, f32[8,256]{1,0:T(8,128)S(1)}, s32[8]{0:T(128)S(1)}, bf16[8,128,128]{2,1,0:T(8,128)(2,1)S(1)}, ...), condition=%wide.region_7.10_spmd, body=%wide.region_4.9_spmd.sunk | while | flops 270532736 | bytes 2266873 | solution.py:28
  186.0 0.7 iota_compare_fusion.13
  186.7 2.3 fusion.46
  190.0 0.7 iota_compare_fusion.13
  190.7 2.3 fusion.46
  193.9 0.7 iota_compare_fusion.13
  194.6 2.3 fusion.46
  198.6 2.3 fusion.46
  201.9 0.7 iota_compare_fusion.13
  202.6 2.3 fusion.46
  205.9 0.7 iota_compare_fusion.13
  206.6 2.3 fusion.46
  209.8 0.7 iota_compare_fusion.13
  210.5 2.3 fusion.46
  214.5 2.3 fusion.46
  217.2 4.7 %collective-permute-start.8 = (f32[256,8]{0,1:T(8,128)S(1)}, f32[256,8]{0,1:T(8,128)S(1)}, u32[]{:S(2)}, u32[]{:S(2)}) collective-permute-start(f32[256,8]{0,1:T(8,128)S(1)} %select_bitcast_fusion.3), channel_id=1, source_target_pairs={{0,7},{1,0},{2,1},{3,2},{4,3},{5,4},{6,5},{7,6},{8,15},{9,8},{10,9... | collective-permute-start | bytes 24584 | tf_op jit(solution)/shard_map/ppermute | solution.py:13
  221.9 2.2 collective-permute-done.9
  224.1 31.8 %while.43 = (s32[]{:T(128)}, f32[8,256]{1,0:T(8,128)S(1)}, s32[8]{0:T(128)S(1)}, bf16[8,128,128]{2,1,0:T(8,128)(2,1)S(1)}, bf16[8192,128]{1,0:T(8,128)(2,1)}, /*index=5*/s32[]{:T(128)}, f32[]{:T(128)}, s32[]{:T(128)}) while((s32[]{:T(128)}, f32[8,256]{1,0:T(8,128)S(1)}, s32[8]{0:T(128)S(1)}, bf16[8,128,128]{2,1,0:T(8,128)(2,1)S(1)}, ...), condition=%wide.region_11.14_spmd, body=%wide.region_8.13_spmd.sunk | while | flops 270532736 | bytes 2266873 | solution.py:28
  225.4 2.3 fusion.49
  229.4 2.3 fusion.49
  233.4 2.3 fusion.49
  237.4 2.3 fusion.49
  241.4 2.3 fusion.49
  245.3 2.3 fusion.49
  249.3 2.3 fusion.49
  253.3 2.3 fusion.49
  256.0 4.3 %collective-permute-done.11 = bf16[8192,128]{1,0:T(8,128)(2,1)S(1)} collective-permute-done((bf16[8192,128]{1,0:T(8,128)(2,1)}, bf16[8192,128]{1,0:T(8,128)(2,1)S(1)}, u32[]{:S(2)}, u32[]{:S(2)}) %collective-permute-start.11) | collective-permute-done | bytes 2097184 | tf_op jit(solution)/shard_map/ppermute | solution.py:13
  260.3 19.0 %while.44 = (s32[]{:T(128)}, f32[8,256]{1,0:T(8,128)S(1)}, s32[8]{0:T(128)S(1)}, bf16[8,128,128]{2,1,0:T(8,128)(2,1)S(1)}, bf16[8192,128]{1,0:T(8,128)(2,1)S(1)}, /*index=5*/s32[]{:T(128)}, f32[]{:T(128)}, s32[]{:T(128)}) while((s32[]{:T(128)}, f32[8,256]{1,0:T(8,128)S(1)}, s32[8]{0:T(128)S(1)}, bf16[8,128,128]{2,1,0:T(8,128)(2,1)S(1)}, ...), condition=%wide.region_15.18_spmd, body=%wide.region_12.17_spmd.sunk | while | flops 270532736 | bytes 2266873 | solution.py:28
  261.6 0.7 fusion.52
  264.0 0.7 fusion.52
  266.4 0.7 fusion.52
  268.7 0.7 fusion.52
  271.1 0.7 fusion.52
  273.5 0.7 fusion.52
  275.8 0.7 fusion.52
  278.2 0.7 fusion.52
  279.4 4.5 %collective-permute-done.12 = f32[256,8]{0,1:T(8,128)S(1)} collective-permute-done((f32[256,8]{0,1:T(8,128)S(1)}, f32[256,8]{0,1:T(8,128)S(1)}, u32[]{:S(2)}, u32[]{:S(2)}) %collective-permute-start.12) | collective-permute-done | bytes 8224 | tf_op jit(solution)/shard_map/ppermute | solution.py:13
  283.8 5.4 %all_gather.23 = f32[256,128]{0,1:T(8,128)S(1)} all-gather(f32[256,32]{0,1:T(8,128)S(1)} %pad_maximum_fusion.1), channel_id=1, replica_groups=mesh['group'=4,'blk'=8] {'group'}, dimensions={1}, use_global_device_ids=true | all-gather | bytes 163840 | tf_op jit(solution)/shard_map/all_gather | solution.py:98
  289.3 3.0 %top_k.9 = (f32[256,128]{0,1:T(8,128)S(1)}, s32[256,128]{0,1:T(8,128)}) sort(f32[256,128]{0,1:T(8,128)S(1)} %all_gather.23, s32[256,128]{0,1:T(8,128)S(1)} %iota.59.clone), dimensions={1}, to_apply=%region_16.19 | sort | flops 491520 | bytes 524288 | tf_op jit(solution)/shard_map/top_k | solution.py:99
  (291 shorter events, 59.4 us)
Async XLA Ops:
  1.4 107.5 %collective-permute-start = (bf16[1,128,128]{2,1,0:T(8,128)(2,1)S(1)}, bf16[1,128,128]{2,1,0:T(8,128)(2,1)S(1)}, u32[]{:S(2)}, u32[]{:S(2)}) collective-permute-start(bf16[1,128,128]{2,1,0:T(8,128)(2,1)S(1)} %select_bitcast_fusion), channel_id=1, source_target_pairs={{0,1},{1,2},{2,3},{3,4},{4,5},{5,6},{6,7},{7,0},{8,9},{9,10},{10,1... | collective-permute-start | bytes 98312 | tf_op jit(solution)/shard_map/ppermute | solution.py:71
  4.4 180.9 %collective-permute-start.7 = (bf16[8192,128]{1,0:T(8,128)(2,1)}, bf16[8192,128]{1,0:T(8,128)(2,1)}, u32[]{:S(2)}, u32[]{:S(2)}) collective-permute-start(bf16[8192,128]{1,0:T(8,128)(2,1)} %bitcast.144), channel_id=1, source_target_pairs={{0,1},{1,2},{2,3},{3,4},{4,5},{5,6},{6,7},{7,0},{8,9},{9,10},{10,1... | collective-permute-start | bytes 6291464 | tf_op jit(solution)/shard_map/ppermute | solution.py:13
  77.2 1.7 copy-start.1
  78.8 30.1 %copy-start.2 = (s32[1,1,2]{2,1,0:T(1,128)S(1)}, s32[1,1,2]{2,1,0:T(1,128)}, u32[]{:S(2)}) copy-start(s32[1,1,2]{2,1,0:T(1,128)} %param.25) | copy-start | bytes 28
  78.8 36.8 %copy-start.3 = (s32[1,1,4]{2,1,0:T(1,128)S(1)}, s32[1,1,4]{2,1,0:T(1,128)}, u32[]{:S(2)}) copy-start(s32[1,1,4]{2,1,0:T(1,128)} %param.23) | copy-start | bytes 52
  78.8 84.8 %copy-start = (bf16[1,16,128,128]{3,2,1,0:T(8,128)(2,1)S(1)}, bf16[1,16,128,128]{3,2,1,0:T(8,128)(2,1)}, u32[]{:S(2)}) copy-start(bf16[1,16,128,128]{3,2,1,0:T(8,128)(2,1)} %param.20) | copy-start | bytes 1572868
  108.8 56.4 %copy-start.4 = (bf16[256,32,128]{2,1,0:T(8,128)(2,1)S(1)}, bf16[256,32,128]{2,1,0:T(8,128)(2,1)}, u32[]{:S(2)}) copy-start(bf16[256,32,128]{2,1,0:T(8,128)(2,1)} %param.19) | copy-start | bytes 6291460
  108.9 6.7 %collective-permute-start.1 = (bf16[1,128,128]{2,1,0:T(8,128)(2,1)S(1)}, bf16[1,128,128]{2,1,0:T(8,128)(2,1)S(1)}, u32[]{:S(2)}, u32[]{:S(2)}) collective-permute-start(bf16[1,128,128]{2,1,0:T(8,128)(2,1)S(1)} %collective-permute-done), channel_id=1, source_target_pairs={{0,1},{1,2},{2,3},{3,4},{4,5},{5,6},{6,7},{7,0},{8,9},{9,10},{10,1... | collective-permute-start | bytes 98312 | tf_op jit(solution)/shard_map/ppermute | solution.py:71
  115.6 21.5 %collective-permute-start.2 = (bf16[1,128,128]{2,1,0:T(8,128)(2,1)S(1)}, bf16[1,128,128]{2,1,0:T(8,128)(2,1)S(1)}, u32[]{:S(2)}, u32[]{:S(2)}) collective-permute-start(bf16[1,128,128]{2,1,0:T(8,128)(2,1)S(1)} %collective-permute-done.1), channel_id=1, source_target_pairs={{0,1},{1,2},{2,3},{3,4},{4,5},{5,6},{6,7},{7,0},{8,9},{9,10},{10,1... | collective-permute-start | bytes 98312 | tf_op jit(solution)/shard_map/ppermute | solution.py:71
  137.1 6.6 %collective-permute-start.3 = (bf16[1,128,128]{2,1,0:T(8,128)(2,1)S(1)}, bf16[1,128,128]{2,1,0:T(8,128)(2,1)S(1)}, u32[]{:S(2)}, u32[]{:S(2)}) collective-permute-start(bf16[1,128,128]{2,1,0:T(8,128)(2,1)S(1)} %collective-permute-done.2), channel_id=1, source_target_pairs={{0,1},{1,2},{2,3},{3,4},{4,5},{5,6},{6,7},{7,0},{8,9},{9,10},{10,1... | collective-permute-start | bytes 98312 | tf_op jit(solution)/shard_map/ppermute | solution.py:71
  143.7 6.6 %collective-permute-start.4 = (bf16[1,128,128]{2,1,0:T(8,128)(2,1)S(1)}, bf16[1,128,128]{2,1,0:T(8,128)(2,1)S(1)}, u32[]{:S(2)}, u32[]{:S(2)}) collective-permute-start(bf16[1,128,128]{2,1,0:T(8,128)(2,1)S(1)} %collective-permute-done.3), channel_id=1, source_target_pairs={{0,1},{1,2},{2,3},{3,4},{4,5},{5,6},{6,7},{7,0},{8,9},{9,10},{10,1... | collective-permute-start | bytes 98312 | tf_op jit(solution)/shard_map/ppermute | solution.py:71
  150.3 6.6 %collective-permute-start.5 = (bf16[1,128,128]{2,1,0:T(8,128)(2,1)S(1)}, bf16[1,128,128]{2,1,0:T(8,128)(2,1)S(1)}, u32[]{:S(2)}, u32[]{:S(2)}) collective-permute-start(bf16[1,128,128]{2,1,0:T(8,128)(2,1)S(1)} %collective-permute-done.4), channel_id=1, source_target_pairs={{0,1},{1,2},{2,3},{3,4},{4,5},{5,6},{6,7},{7,0},{8,9},{9,10},{10,1... | collective-permute-start | bytes 98312 | tf_op jit(solution)/shard_map/ppermute | solution.py:71
  156.9 6.6 %collective-permute-start.6 = (bf16[1,128,128]{2,1,0:T(8,128)(2,1)S(1)}, bf16[1,128,128]{2,1,0:T(8,128)(2,1)S(1)}, u32[]{:S(2)}, u32[]{:S(2)}) collective-permute-start(bf16[1,128,128]{2,1,0:T(8,128)(2,1)S(1)} %collective-permute-done.5), channel_id=1, source_target_pairs={{0,1},{1,2},{2,3},{3,4},{4,5},{5,6},{6,7},{7,0},{8,9},{9,10},{10,1... | collective-permute-start | bytes 98312 | tf_op jit(solution)/shard_map/ppermute | solution.py:71
  185.2 38.8 %collective-permute-start.9 = (bf16[8192,128]{1,0:T(8,128)(2,1)}, bf16[8192,128]{1,0:T(8,128)(2,1)}, u32[]{:S(2)}, u32[]{:S(2)}) collective-permute-start(bf16[8192,128]{1,0:T(8,128)(2,1)} %collective-permute-done.7), channel_id=1, source_target_pairs={{0,1},{1,2},{2,3},{3,4},{4,5},{5,6},{6,7},{7,0},{8,9},{9,10},{10,1... | collective-permute-start | bytes 6291464 | tf_op jit(solution)/shard_map/ppermute | solution.py:13
  217.2 62.2 %collective-permute-start.8 = (f32[256,8]{0,1:T(8,128)S(1)}, f32[256,8]{0,1:T(8,128)S(1)}, u32[]{:S(2)}, u32[]{:S(2)}) collective-permute-start(f32[256,8]{0,1:T(8,128)S(1)} %select_bitcast_fusion.3), channel_id=1, source_target_pairs={{0,7},{1,0},{2,1},{3,2},{4,3},{5,4},{6,5},{7,6},{8,15},{9,8},{10,9... | collective-permute-start | bytes 24584 | tf_op jit(solution)/shard_map/ppermute | solution.py:13
  224.1 36.2 %collective-permute-start.11 = (bf16[8192,128]{1,0:T(8,128)(2,1)}, bf16[8192,128]{1,0:T(8,128)(2,1)S(1)}, u32[]{:S(2)}, u32[]{:S(2)}) collective-permute-start(bf16[8192,128]{1,0:T(8,128)(2,1)} %collective-permute-done.9), channel_id=1, source_target_pairs={{0,1},{1,2},{2,3},{3,4},{4,5},{5,6},{6,7},{7,0},{8,9},{9,10},{10,1... | collective-permute-start | bytes 6291464 | tf_op jit(solution)/shard_map/ppermute | solution.py:13
  256.0 23.4 %collective-permute-start.10 = (f32[256,8]{0,1:T(8,128)S(1)}, f32[256,8]{0,1:T(8,128)S(1)}, u32[]{:S(2)}, u32[]{:S(2)}) collective-permute-start(f32[256,8]{0,1:T(8,128)S(1)} %select_bitcast_fusion.2), channel_id=1, source_target_pairs={{0,6},{1,7},{2,0},{3,1},{4,2},{5,3},{6,4},{7,5},{8,14},{9,15},{10,... | collective-permute-start | bytes 24584 | tf_op jit(solution)/shard_map/ppermute | solution.py:13
  279.3 4.5 %collective-permute-start.12 = (f32[256,8]{0,1:T(8,128)S(1)}, f32[256,8]{0,1:T(8,128)S(1)}, u32[]{:S(2)}, u32[]{:S(2)}) collective-permute-start(f32[256,8]{0,1:T(8,128)S(1)} %select_bitcast_fusion.1), channel_id=1, source_target_pairs={{0,5},{1,6},{2,7},{3,0},{4,1},{5,2},{6,3},{7,4},{8,13},{9,14},{10,... | collective-permute-start | bytes 24584 | tf_op jit(solution)/shard_map/ppermute | solution.py:13
